TPU v7x, 32 devices: a whole 2x2x4 slice. The times are simulated.
32 devices in a mesh: feat: 8 (over z, y), tok: 4 (over x, core).
Axes of the slice: x: 2, y: 2, z: 4, core: 2. Of those that a mesh axis runs over, the one named last changes fastest.
Arguments:
- activations: bfloat16 [2560, 13312], P('tok', 'feat'), may hold values from -18 to 18
- hessian: float32 [64, 1664, 1664], P('feat', 'tok'), may hold values from -6 to 6
Outputs:
- updated: float32 [64, 1664, 1664], P('feat', 'tok')
All inputs are finite; a program needn't handle non-finite values.
Results may differ from a plain program's by a relative error of at most 0.0003.
Values may be sent and summed in bfloat16 or wider, within the bound.
A program may use at most 256 MiB of HBM per device.

v0:
```python
import jax
import jax.numpy as jnp
from jax import lax
from jax.sharding import PartitionSpec as P

TILES = 8


def contract_tokens(left, right):
    return lax.dot_general(
        left, right, (((0,), (0,)), ((), ())), preferred_element_type=jnp.float32
    )


def tile_sums(row_block, col_block, lower_tile):
    width = row_block.shape[1]
    quarter_width = col_block.shape[1] // lax.axis_size("tok")
    every_rows = lax.all_gather(row_block, "tok", axis=0, tiled=True)
    every_cols = lax.all_to_all(col_block, "tok", split_axis=1, concat_axis=0, tiled=True)
    return lax.cond(
        lower_tile,
        lambda: contract_tokens(every_cols, every_rows),
        lambda: jnp.zeros((quarter_width, width), jnp.float32),
    )


def on_device(activations, hessian):
    tok_count = lax.axis_size("tok")
    total_tokens = activations.shape[0] * tok_count
    seen_tokens = 2 * total_tokens
    seen_share = seen_tokens / (seen_tokens + total_tokens)
    weight_new = 2.0 / (seen_tokens + total_tokens)
    position = lax.axis_index("feat")
    tok_position = lax.axis_index("tok")
    local_tiles = hessian.shape[0]
    quarter_width = hessian.shape[1]
    width = hessian.shape[2]
    gathered = lax.all_gather(activations, "feat", axis=1, tiled=True)
    results = []
    for slot in range(local_tiles):
        tile_index = position * local_tiles + slot
        row_tile = tile_index // TILES
        col_tile = tile_index % TILES
        row_block = lax.dynamic_slice_in_dim(gathered, row_tile * width, width, 1)
        col_block = lax.dynamic_slice_in_dim(gathered, col_tile * width, width, 1)
        sums = tile_sums(row_block, col_block, row_tile >= col_tile)
        row_ids = row_tile * width + jnp.arange(width, dtype=jnp.int32)
        col_ids = (
            col_tile * width
            + tok_position * quarter_width
            + jnp.arange(quarter_width, dtype=jnp.int32)
        )
        lower = row_ids[None, :] >= col_ids[:, None]
        previous = hessian[slot]
        results.append(jnp.where(lower, seen_share * previous + weight_new * sums, previous))
    return jnp.stack(results)


def solution(mesh):
    in_specs = (P("tok", "feat"), P("feat", "tok", None))
    out_specs = P("feat", "tok", None)
    return jax.shard_map(
        on_device, mesh=mesh, in_specs=in_specs, out_specs=out_specs, check_vma=False
    )
```

profile of v0, /device:TPU:28, one launch (start us, length us, event | category | flops | bytes accessed | tf_op | source)
XLA Modules:
  0.0 1053.6 jit_solution(10586810755513142803)
XLA Ops:
  6.5 4.1 copy.3
  10.6 0.0 all-gather.14.cloned.1.call-start
  10.9 327.7 %all-gather.10.cloned.1.call-done = bf16[640,13312]{0,1:T(8,128)(2,1)} async-done(((bf16[640,1664]{0,1:T(8,128)(2,1)}), bf16[640,13312]{0,1:T(8,128)(2,1)}) %all-gather.10.cloned.1.call-update) | async-done | bytes 17039376 | tf_op jit(solution)/shard_map/all_gather | solution.py:38
  338.6 25.9 %constant_dynamic-slice_fusion = (bf16[640,1664]{0,1:T(8,128)(2,1)}, bf16[640,1664]{0,1:T(8,128)(2,1)}, bf16[640,1664]{0,1:T(8,128)(2,1)}, bf16[640,1664]{0,1:T(...) fusion(bf16[640,13312]{0,1:T(8,128)(2,1)} %all-gather.10.cloned, ...), kind=kLoop, calls=%fused_computation.40 | loop fusion | bytes 68157504 | tf_op jit(solution)/shard_map/dynamic_slice | solution.py:44
  364.5 0.0 all-gather.12.cloned.1.call-start
  364.5 0.7 all-gather.12.cloned.1.call-update
  365.3 0.5 all-gather.16.cloned.1.call-update
  365.8 0.5 all-gather.18.cloned.1.call-update
  366.4 0.5 all-gather.20.cloned.1.call-update
  367.0 0.7 all-gather.22.cloned.1.call-update
  367.7 0.7 all-gather.24.cloned.1.call-update
  368.4 4.5 all-to-all-start.1
  373.0 0.7 all-gather.26.cloned.1.call-update
  373.7 46.5 %all-to-all-done.1 = bf16[640,4,416]{0,2,1:T(8,128)(2,1)} async-done(((bf16[640,4,416]{0,2,1:T(8,128)(2,1)}), bf16[640,4,416]{0,2,1:T(8,128)(2,1)}, u32[]{:S(2)}, u32[]{:S(2)}) %all-to-all-start.1) | async-done | bytes 2129952 | tf_op jit(solution)/shard_map/all_to_all | solution.py:19
  420.2 47.3 %all_to_all.152 = bf16[640,4,416]{0,2,1:T(8,128)(2,1)} all-to-all(bf16[640,4,416]{0,2,1:T(8,128)(2,1)} %bitcast.132), channel_id=1, replica_groups=mesh['feat'=8,'tok'=4] {'tok'}, dimensions={1} | all-to-all | bytes 4259840 | tf_op jit(solution)/shard_map/all_to_all | solution.py:19
  467.5 50.5 %all_to_all.153 = bf16[640,4,416]{0,2,1:T(8,128)(2,1)} all-to-all(bf16[640,4,416]{0,2,1:T(8,128)(2,1)S(1)} %bitcast.131), channel_id=1, replica_groups=mesh['feat'=8,'tok'=4] {'tok'}, dimensions={1} | all-to-all | bytes 4259840 | tf_op jit(solution)/shard_map/all_to_all | solution.py:19
  518.1 47.4 %all_to_all.154 = bf16[640,4,416]{0,2,1:T(8,128)(2,1)} all-to-all(bf16[640,4,416]{0,2,1:T(8,128)(2,1)S(1)} %bitcast.130), channel_id=1, replica_groups=mesh['feat'=8,'tok'=4] {'tok'}, dimensions={1} | all-to-all | bytes 4259840 | tf_op jit(solution)/shard_map/all_to_all | solution.py:19
  565.4 49.2 %all_to_all.155 = bf16[640,4,416]{0,2,1:T(8,128)(2,1)} all-to-all(bf16[640,4,416]{0,2,1:T(8,128)(2,1)S(1)} %bitcast.129), channel_id=1, replica_groups=mesh['feat'=8,'tok'=4] {'tok'}, dimensions={1} | all-to-all | bytes 4259840 | tf_op jit(solution)/shard_map/all_to_all | solution.py:19
  614.6 48.5 %all_to_all.156 = bf16[640,4,416]{0,2,1:T(8,128)(2,1)} all-to-all(bf16[640,4,416]{0,2,1:T(8,128)(2,1)S(1)} %bitcast.128), channel_id=1, replica_groups=mesh['feat'=8,'tok'=4] {'tok'}, dimensions={1} | all-to-all | bytes 4259840 | tf_op jit(solution)/shard_map/all_to_all | solution.py:19
  663.1 3.6 all-to-all-start.6
  666.8 45.0 %all-to-all-done.6 = bf16[640,4,416]{0,2,1:T(8,128)(2,1)S(1)} async-done(((bf16[640,4,416]{0,2,1:T(8,128)(2,1)}), bf16[640,4,416]{0,2,1:T(8,128)(2,1)S(1)}, u32[]{:S(2)}, u32[]{:S(2)}) %all-to-all-start.6) | async-done | bytes 2129952 | tf_op jit(solution)/shard_map/all_to_all | solution.py:19
  711.8 4.5 all-to-all-start.7
  716.6 13.6 %conditional.9 = (f32[416,1664]{1,0:T(8,128)S(1)}) conditional(s32[]{:T(128)} %convert_element_type.25, () %tuple.55, (bf16[4,640,416]{1,2,0:T(8,128)(2,1)}, bf16[2560,1664]{0,1:T(8,128)(2,1)}) %tuple.56), branch_computations={%region_2.3_spmd, %region_3.4_spmd} | conditional | flops 3544186880 | bytes 17678344 | solution.py:20
  716.7 4.3 copy.6
  720.9 9.3 fusion.9
  730.2 15.5 %conditional.8 = (f32[416,1664]{1,0:T(8,128)}) conditional(s32[]{:T(128)} %convert_element_type.24, () %tuple.53, (bf16[4,640,416]{1,2,0:T(8,128)(2,1)}, bf16[2560,1664]{0,1:T(8,128)(2,1)}) %tuple.131), branch_computations={%region_0.1_spmd, %region_1.2_spmd} | conditional | flops 3544186880 | bytes 17678344 | solution.py:20
  730.7 4.3 copy.4
  735.0 10.7 %fusion.8 = f32[416,1664]{1,0:T(8,128)} fusion(bf16[2560,416]{1,0:T(8,128)(2,1)} %bitcast.141, bf16[2560,1664]{0,1:T(8,128)(2,1)} %get-tuple-element.86), kind=kOutput, calls=%fused_computation.64 | convolution fusion | flops 3544186880 | bytes 13418496 | tf_op jit(solution)/shard_map/cond/branch_1_fun/dot_general | solution.py:10
  745.8 15.1 %conditional.10 = (f32[416,1664]{1,0:T(8,128)}) conditional(s32[]{:T(128)} %convert_element_type.26, () %tuple.57, (bf16[4,640,416]{1,2,0:T(8,128)(2,1)}, bf16[2560,1664]{0,1:T(8,128)(2,1)}) %tuple.130), branch_computations={%region_4.5_spmd, %region_5.6_spmd} | conditional | flops 3544186880 | bytes 17678344 | solution.py:20
  745.8 4.3 copy.8
  750.1 10.8 %fusion.10 = f32[416,1664]{1,0:T(8,128)} fusion(bf16[2560,416]{1,0:T(8,128)(2,1)} %bitcast.142, bf16[2560,1664]{0,1:T(8,128)(2,1)} %get-tuple-element.90), kind=kOutput, calls=%fused_computation.66 | convolution fusion | flops 3544186880 | bytes 13418496 | tf_op jit(solution)/shard_map/cond/branch_1_fun/dot_general | solution.py:10
  760.9 16.6 %conditional.11 = (f32[416,1664]{1,0:T(8,128)}) conditional(s32[]{:T(128)} %convert_element_type.27, () %tuple.59, (bf16[4,640,416]{1,2,0:T(8,128)(2,1)}, bf16[2560,1664]{0,1:T(8,128)(2,1)}) %tuple.129), branch_computations={%region_6.7_spmd, %region_7.8_spmd} | conditional | flops 3544186880 | bytes 17678344 | solution.py:20
  761.0 4.3 copy.10
  765.3 12.1 %fusion.11 = f32[416,1664]{1,0:T(8,128)} fusion(bf16[2560,416]{1,0:T(8,128)(2,1)} %bitcast.143, bf16[2560,1664]{0,1:T(8,128)(2,1)} %get-tuple-element.92), kind=kOutput, calls=%fused_computation.67 | convolution fusion | flops 3544186880 | bytes 13418496 | tf_op jit(solution)/shard_map/cond/branch_1_fun/dot_general | solution.py:10
  777.4 41.9 %all-gather.20.cloned.1.call-done = bf16[2560,1664]{0,1:T(8,128)(2,1)} async-done(((bf16[640,1664]{0,1:T(8,128)(2,1)}), bf16[2560,1664]{0,1:T(8,128)(2,1)}) %all-gather.20.cloned.1.call-update) | async-done | bytes 8519696 | tf_op jit(solution)/shard_map/all_gather | solution.py:18
  819.3 15.4 %conditional.12 = (f32[416,1664]{1,0:T(8,128)}) conditional(s32[]{:T(128)} %convert_element_type.28, () %tuple.61, (bf16[4,640,416]{1,2,0:T(8,128)(2,1)}, bf16[2560,1664]{0,1:T(8,128)(2,1)}) %tuple.128), branch_computations={%region_8.9_spmd, %region_9.10_spmd} | conditional | flops 3544186880 | bytes 17678344 | solution.py:20
  819.3 4.3 copy.12
  823.6 11.1 %fusion.12 = f32[416,1664]{1,0:T(8,128)} fusion(bf16[2560,416]{1,0:T(8,128)(2,1)} %bitcast.144, bf16[2560,1664]{0,1:T(8,128)(2,1)} %get-tuple-element.94), kind=kOutput, calls=%fused_computation.68 | convolution fusion | flops 3544186880 | bytes 13418496 | tf_op jit(solution)/shard_map/cond/branch_1_fun/dot_general | solution.py:10
  834.7 45.2 %all-gather.22.cloned.1.call-done = bf16[2560,1664]{0,1:T(8,128)(2,1)} async-done(((bf16[640,1664]{0,1:T(8,128)(2,1)}), bf16[2560,1664]{0,1:T(8,128)(2,1)}) %all-gather.22.cloned.1.call-update) | async-done | bytes 8519696 | tf_op jit(solution)/shard_map/all_gather | solution.py:18
  879.8 15.5 %conditional.13 = (f32[416,1664]{1,0:T(8,128)}) conditional(s32[]{:T(128)} %convert_element_type.29, () %tuple.63, (bf16[4,640,416]{1,2,0:T(8,128)(2,1)}, bf16[2560,1664]{0,1:T(8,128)(2,1)}) %tuple.127), branch_computations={%region_10.11_spmd, %region_11.12_spmd} | conditional | flops 3544186880 | bytes 17678344 | solution.py:20
  880.0 4.3 copy.14
  884.3 11.1 %fusion.13 = f32[416,1664]{1,0:T(8,128)} fusion(bf16[2560,416]{1,0:T(8,128)(2,1)} %bitcast.145, bf16[2560,1664]{0,1:T(8,128)(2,1)} %get-tuple-element.96), kind=kOutput, calls=%fused_computation.69 | convolution fusion | flops 3544186880 | bytes 13418496 | tf_op jit(solution)/shard_map/cond/branch_1_fun/dot_general | solution.py:10
  895.4 45.0 %all-gather.24.cloned.1.call-done = bf16[2560,1664]{0,1:T(8,128)(2,1)} async-done(((bf16[640,1664]{0,1:T(8,128)(2,1)}), bf16[2560,1664]{0,1:T(8,128)(2,1)}) %all-gather.24.cloned.1.call-update) | async-done | bytes 8519696 | tf_op jit(solution)/shard_map/all_gather | solution.py:18
  940.4 15.3 %conditional.14 = (f32[416,1664]{1,0:T(8,128)}) conditional(s32[]{:T(128)} %convert_element_type.30, () %tuple.65, (bf16[4,640,416]{1,2,0:T(8,128)(2,1)}, bf16[2560,1664]{0,1:T(8,128)(2,1)}) %tuple.126), branch_computations={%region_12.13_spmd, %region_13.14_spmd} | conditional | flops 3544186880 | bytes 17678344 | solution.py:20
  940.4 4.3 copy.16
  944.7 11.0 %fusion.14 = f32[416,1664]{1,0:T(8,128)} fusion(bf16[2560,416]{1,0:T(8,128)(2,1)} %bitcast.146, bf16[2560,1664]{0,1:T(8,128)(2,1)} %get-tuple-element.98), kind=kOutput, calls=%fused_computation.70 | convolution fusion | flops 3544186880 | bytes 13418496 | tf_op jit(solution)/shard_map/cond/branch_1_fun/dot_general | solution.py:10
  955.7 45.3 %all-gather.26.cloned.1.call-done = bf16[2560,1664]{0,1:T(8,128)(2,1)} async-done(((bf16[640,1664]{0,1:T(8,128)(2,1)}), bf16[2560,1664]{0,1:T(8,128)(2,1)}) %all-gather.26.cloned.1.call-update) | async-done | bytes 8519696 | tf_op jit(solution)/shard_map/all_gather | solution.py:18
  1001.0 15.2 %conditional.15 = (f32[416,1664]{1,0:T(8,128)}) conditional(s32[]{:T(128)} %convert_element_type.31, () %tuple.67, (bf16[4,640,416]{1,2,0:T(8,128)(2,1)}, bf16[2560,1664]{0,1:T(8,128)(2,1)}) %tuple.68), branch_computations={%region_14.15_spmd, %region_15.16_spmd} | conditional | flops 3544186880 | bytes 17678344 | solution.py:20
  1001.2 4.3 copy.18
  1005.5 10.7 %fusion.15 = f32[416,1664]{1,0:T(8,128)} fusion(bf16[2560,416]{1,0:T(8,128)(2,1)} %bitcast.147, bf16[2560,1664]{0,1:T(8,128)(2,1)} %get-tuple-element.100), kind=kOutput, calls=%fused_computation.71 | convolution fusion | flops 3544186880 | bytes 13418496 | tf_op jit(solution)/shard_map/cond/branch_1_fun/dot_general | solution.py:10
  1016.2 3.2 bitcast_dynamic-update-slice_fusion.7
  1019.4 2.4 bitcast_dynamic-update-slice_fusion.6
  1021.8 0.2 copy-done
  1022.0 2.5 bitcast_dynamic-update-slice_fusion.5
  1024.4 0.2 copy-done.1
  1024.6 2.4 bitcast_dynamic-update-slice_fusion.4
  1027.0 0.2 copy-done.2
  1027.2 2.5 bitcast_dynamic-update-slice_fusion.3
  1029.7 0.2 copy-done.3
  1029.8 2.4 bitcast_dynamic-update-slice_fusion.2
  1032.3 0.2 copy-done.4
  1032.4 2.5 bitcast_dynamic-update-slice_fusion.1
  1034.9 7.9 copy-done.10
  1042.8 3.8 bitcast_dynamic-update-slice_fusion
  (46 shorter events, 0.4 us)
Async XLA Ops:
  6.5 332.0 %all-gather.10.cloned.1.call-start = ((), (), s32[]{:S(2)}) async-start(), calls=%async_computation.8 | async-start | bytes 19169280 | tf_op jit(solution)/shard_map/all_gather | solution.py:38
  10.6 706.0 %all-gather.14.cloned.1.call-start = ((), (), s32[]{:S(2)}) async-start(), calls=%async_computation.10 | async-start | bytes 10649600 | tf_op jit(solution)/shard_map/all_gather | solution.py:18
  364.5 365.8 %all-gather.12.cloned.1.call-start = ((), (), s32[]{:S(2)}) async-start(), calls=%async_computation.9 | async-start | bytes 10649600 | tf_op jit(solution)/shard_map/all_gather | solution.py:18
  365.2 380.5 %all-gather.16.cloned.1.call-start = ((), (), s32[]{:S(2)}) async-start(), calls=%async_computation.11 | async-start | bytes 10649600 | tf_op jit(solution)/shard_map/all_gather | solution.py:18
  365.8 395.1 %all-gather.18.cloned.1.call-start = ((), (), s32[]{:S(2)}) async-start(), calls=%async_computation.12 | async-start | bytes 10649600 | tf_op jit(solution)/shard_map/all_gather | solution.py:18
  366.4 452.9 %all-gather.20.cloned.1.call-start = ((), (), s32[]{:S(2)}) async-start(), calls=%async_computation.13 | async-start | bytes 10649600 | tf_op jit(solution)/shard_map/all_gather | solution.py:18
  366.9 512.9 %all-gather.22.cloned.1.call-start = ((), (), s32[]{:S(2)}) async-start(), calls=%async_computation.14 | async-start | bytes 10649600 | tf_op jit(solution)/shard_map/all_gather | solution.py:18
  367.7 572.7 %all-gather.24.cloned.1.call-start = ((), (), s32[]{:S(2)}) async-start(), calls=%async_computation.15 | async-start | bytes 10649600 | tf_op jit(solution)/shard_map/all_gather | solution.py:18
  368.4 51.7 %all-to-all-start.1 = ((bf16[640,4,416]{0,2,1:T(8,128)(2,1)}), bf16[640,4,416]{0,2,1:T(8,128)(2,1)}, u32[]{:S(2)}, u32[]{:S(2)}) async-start(bf16[640,4,416]{0,2,1:T(8,128)(2,1)} %bitcast.133), calls=%async_computation.1 | async-start | bytes 4259840 | tf_op jit(solution)/shard_map/all_to_all | solution.py:19
  372.9 628.0 %all-gather.26.cloned.1.call-start = ((), (), s32[]{:S(2)}) async-start(), calls=%async_computation.16 | async-start | bytes 10649600 | tf_op jit(solution)/shard_map/all_gather | solution.py:18
  420.2 47.3 %copy-start.8 = (bf16[640,1664]{0,1:T(8,128)(2,1)S(1)}, bf16[640,1664]{0,1:T(8,128)(2,1)}, u32[]{:S(2)}) copy-start(bf16[640,1664]{0,1:T(8,128)(2,1)} %get-tuple-element.112) | copy-start | bytes 6389764
  467.5 50.5 %copy-start.7 = (bf16[640,1664]{0,1:T(8,128)(2,1)S(1)}, bf16[640,1664]{0,1:T(8,128)(2,1)}, u32[]{:S(2)}) copy-start(bf16[640,1664]{0,1:T(8,128)(2,1)} %get-tuple-element.110) | copy-start | bytes 6389764
  518.0 47.4 %copy-start.6 = (bf16[640,1664]{0,1:T(8,128)(2,1)S(1)}, bf16[640,1664]{0,1:T(8,128)(2,1)}, u32[]{:S(2)}) copy-start(bf16[640,1664]{0,1:T(8,128)(2,1)} %get-tuple-element.108) | copy-start | bytes 6389764
  663.1 48.7 %all-to-all-start.6 = ((bf16[640,4,416]{0,2,1:T(8,128)(2,1)}), bf16[640,4,416]{0,2,1:T(8,128)(2,1)S(1)}, u32[]{:S(2)}, u32[]{:S(2)}) async-start(bf16[640,4,416]{0,2,1:T(8,128)(2,1)} %bitcast.33), calls=%async_computation.6 | async-start | bytes 4259840 | tf_op jit(solution)/shard_map/all_to_all | solution.py:19
  711.8 4.8 copy-start.9
  711.8 243.8 %all-to-all-start.7 = ((bf16[640,4,416]{0,2,1:T(8,128)(2,1)}), bf16[640,4,416]{0,2,1:T(8,128)(2,1)}, u32[]{:S(2)}, u32[]{:S(2)}) async-start(bf16[640,4,416]{0,2,1:T(8,128)(2,1)} %bitcast.37), calls=%async_computation.7 | async-start | bytes 4259840 | tf_op jit(solution)/shard_map/all_to_all | solution.py:19
  1019.4 2.6 copy-start
  1022.0 2.6 copy-start.1
  1024.6 2.6 copy-start.2
  1027.2 2.6 copy-start.3
  1029.8 2.6 copy-start.4
  1032.4 10.4 copy-start.5
  1034.9 7.9 copy-start.10
Sparse Core Ops, SparseCore 0:
  10.7 327.7 all-gather.9
  364.6 98.2 all-gather.13
  464.4 97.4 all-gather.11
  563.3 97.6 all-gather.15
  662.4 96.3 all-gather.17
  760.3 58.9 all-gather.19
  820.8 58.9 all-gather.21
  881.4 58.9 all-gather.23
  942.0 58.9 all-gather.25
where the time goes:
time: 1060 us; the launch traced here: 1050 us
  waiting for transfers between devices  601 us (57%)
  blocking collectives  243 us (23%)
  matrix products  86.6 us (8%)
  local copies, waits for them, and re-layouts  73.1 us (7%)
  other arithmetic  21.8 us (2%)
  between operations  14.1 us (1%)
  starting transfers between devices  12.9 us (1%)
    all_gather x1, waiting for transfers between devices, on_device(): gathered = lax.all_gather(activations, 'feat', axis=1, tiled=True)  328 us
    all_to_all x5, blocking collectives, tile_sums(): lax.all_to_all(col_block, 'tok', split_axis=1, concat_axis=0, tiled=True)  243 us
    all_gather x8, waiting for transfers between devices, tile_sums(): every_rows = lax.all_gather(row_block, 'tok', axis=0, tiled=True)  177 us
    all_to_all x3, waiting for transfers between devices, tile_sums(): lax.all_to_all(col_block, 'tok', split_axis=1, concat_axis=0, tiled=True)  91.5 us
    dot_general x8, matrix products, contract_tokens(): lax.dot_general(left, right, (((0,), (0,)), ((), ())), preferred_element_...  86.6 us
    another operation x8, local copies, waits for them, and re-layouts  34.4 us
    dynamic_slice x1, local copies, waits for them, and re-layouts, on_device(): row_block = lax.dynamic_slice_in_dim(gathered, row_tile * width, width, 1)  25.9 us
  transfers between devices with their start and end apart: 12, of which 7 were waited for; matrix products, arithmetic and copies ran while one was open for 10% of the time, Pallas kernels for 0%

commit v1 on v0

--- a/solution.py
+++ b/solution.py
@@ -1,9 +1,12 @@
 import jax
 import jax.numpy as jnp
 from jax import lax
+from jax.experimental import pallas as pl
+from jax.experimental.pallas import tpu as pltpu
 from jax.sharding import PartitionSpec as P
 
 TILES = 8
+MESH = pl.DeviceIdType.MESH
 
 
 def contract_tokens(left, right):
@@ -24,12 +27,14 @@
     )
 
 
-def on_device(activations, hessian):
-    tok_count = lax.axis_size("tok")
-    total_tokens = activations.shape[0] * tok_count
+def shares(activations):
+    total_tokens = activations.shape[0] * lax.axis_size("tok")
     seen_tokens = 2 * total_tokens
-    seen_share = seen_tokens / (seen_tokens + total_tokens)
-    weight_new = 2.0 / (seen_tokens + total_tokens)
+    return seen_tokens / (seen_tokens + total_tokens), 2.0 / (seen_tokens + total_tokens)
+
+
+def on_device_general(activations, hessian):
+    seen_share, weight_new = shares(activations)
     position = lax.axis_index("feat")
     tok_position = lax.axis_index("tok")
     local_tiles = hessian.shape[0]
@@ -56,6 +61,229 @@
     return jnp.stack(results)
 
 
+def share_kernel(feat, tok, a_ref, at_ref, cols, rows, up_sem, side_sem, swap_sem, in_sem,
+                 row_send, row_in, local_sem):
+    p = lax.axis_index("feat")
+    t = lax.axis_index("tok")
+    y = p % 2
+    z = p // 2
+    last_z = feat // 2 - 1
+    up = p + 2
+    side = p + 1 - 2 * y
+    near = [t, t + 1 - 2 * (t % 2), (t + 2) % 4, 3 - t]
+    tokens, width = a_ref.shape
+    quarter = width // tok
+    has_up = z < last_z
+
+    barrier = pltpu.get_barrier_semaphore()
+    for r in (1, 2, 3):
+        pl.semaphore_signal(barrier, inc=1, device_id=(p, near[r]), device_id_type=MESH)
+    pl.semaphore_signal(barrier, inc=1, device_id=(side, t), device_id_type=MESH)
+
+    @pl.when(has_up)
+    def _():
+        pl.semaphore_signal(barrier, inc=1, device_id=(up, t), device_id_type=MESH)
+
+    @pl.when(z > 0)
+    def _():
+        pl.semaphore_signal(barrier, inc=1, device_id=(p - 2, t), device_id_type=MESH)
+
+    pl.semaphore_wait(barrier, 4 + has_up.astype(jnp.int32) + (z > 0).astype(jnp.int32))
+
+    def block(j, who):
+        return cols.at[j, :, pl.ds(pl.multiple_of(who * tokens, tokens), tokens)]
+
+    def mine(who):
+        return at_ref.at[pl.ds(pl.multiple_of(who * quarter, quarter), quarter), :]
+
+    def row_block(who):
+        return rows.at[pl.ds(pl.multiple_of(who * tokens, tokens), tokens), :]
+
+    def move(src, j, who, send, device):
+        return pltpu.make_async_remote_copy(
+            src_ref=src, dst_ref=block(j, who), send_sem=send, recv_sem=in_sem.at[j, who],
+            device_id=device, device_id_type=MESH)
+
+    def arrive(j, r):
+        move(block(j, near[r]), j, near[r], up_sem.at[j, r], (side, t)).wait_recv()
+
+    def send_row(src, who, index, device):
+        return pltpu.make_async_remote_copy(
+            src_ref=src, dst_ref=row_block(who), send_sem=row_send.at[index],
+            recv_sem=row_in.at[who], device_id=device, device_id_type=MESH)
+
+    ended = []
+
+    def start_if(cond, copy):
+        @pl.when(cond)
+        def _():
+            copy.start()
+        ended.append((cond, copy))
+
+    def lane(even, r, j):
+        if even:
+            return r % 2 + 0 * j
+        return jnp.where((r == 3) | ((r == 2) & (j == feat - 3)), 0, 1)
+
+    def forward_up(j, r, lane_of, src=None):
+        src = block(j, near[r]) if src is None else src
+        start_if(has_up & (lane_of == y), move(src, j, near[r], up_sem.at[j, r], (up, t)))
+
+    swaps = [move(mine(near[r]), p, t, swap_sem.at[r], (p, near[r])) for r in (2, 3, 1)]
+    for copy in swaps:
+        copy.start()
+    own_cols = pltpu.make_async_copy(mine(t), block(p, t), local_sem.at[0])
+    own_rows = pltpu.make_async_copy(a_ref, row_block(t), local_sem.at[1])
+    own_lane = [jnp.where(y == 0, r % 2, lane(False, r, p)) for r in range(4)]
+    side_lane = [jnp.where(y == 1, r % 2, lane(False, r, side)) for r in range(4)]
+    row_sends = [send_row(a_ref, t, 0, (p, near[2])), send_row(a_ref, t, 1, (p, near[1]))]
+
+    for r in range(4):
+        if r:
+            arrive(p, r)
+        src = mine(t) if r == 0 else None
+        forward_up(p, r, own_lane[r], src)
+        start_if((y == 0) | (has_up & (own_lane[r] == 0)),
+                 move(block(p, near[r]) if src is None else src, p, near[r],
+                      side_sem.at[p, r], (side, t)))
+        if r == 0:
+            own_cols.start()
+            own_rows.start()
+        if r == 1:
+            for copy in row_sends:
+                copy.start()
+
+    for r in range(4):
+        @pl.when((y == 1) | (has_up & (side_lane[r] == 0)))
+        def _():
+            arrive(side, r)
+        forward_up(side, r, side_lane[r])
+
+    pass_row = send_row(row_block(near[2]), near[2], 2, (p, near[1]))
+
+    def pass_rows():
+        send_row(row_block(near[2]), near[2], 2, (p, near[2])).wait_recv()
+        pass_row.start()
+
+    own_rows.wait()
+    for dz in range(1, last_z + 1):
+        for even in (True, False):
+            for r in range(4):
+                j = jnp.maximum(2 * (z - dz) + (0 if even else 1), 0)
+                here = lane(even, r, j) == y
+                cond = (z >= dz) & here
+
+                @pl.when(cond)
+                def _():
+                    arrive(j, r)
+                start_if(cond & has_up, move(block(j, near[r]), j, near[r], up_sem.at[j, r], (up, t)))
+                start_if(cond, move(block(j, near[r]), j, near[r], side_sem.at[j, r], (side, t)))
+        if dz == 1:
+            pass_rows()
+
+    for dz in range(1, last_z + 1):
+        for even in (True, False):
+            for r in range(4):
+                j = jnp.maximum(2 * (z - dz) + (0 if even else 1), 0)
+
+                @pl.when((z >= dz) & (lane(even, r, j) != y))
+                def _():
+                    arrive(j, r)
+
+    for r in (1, 3):
+        send_row(row_block(near[r]), near[r], 2, (p, near[1])).wait_recv()
+    own_cols.wait()
+    for copy in swaps + row_sends + [pass_row]:
+        copy.wait_send()
+    for cond, copy in ended:
+        @pl.when(cond)
+        def _():
+            copy.wait_send()
+
+
+def blend_kernel(seen_share, weight_new, pos, cols, rows, h, out):
+    j = pl.program_id(0)
+    width = rows.shape[1]
+    quarter = h.shape[1]
+
+    def part(start, size):
+        at = pl.ds(start, size)
+        sums = jnp.dot(cols[0], rows[:, at], preferred_element_type=jnp.float32)
+        old = h[0, :, at]
+        row_ids = pos[0] * width + start + lax.broadcasted_iota(jnp.int32, (1, size), 1)
+        col_ids = j * width + pos[1] * quarter + lax.broadcasted_iota(jnp.int32, (quarter, 1), 0)
+        out[0, :, at] = jnp.where(row_ids >= col_ids, seen_share * old + weight_new * sums, old)
+
+    @pl.when(j <= pos[0])
+    def _():
+        step = 256
+        @pl.loop(0, width // step)
+        def _(i):
+            part(pl.multiple_of(i * step, step), step)
+        if width % step:
+            part(width // step * step, width % step)
+
+    @pl.when(j > pos[0])
+    def _():
+        out[...] = h[...]
+
+
+def on_device_panels(activations, hessian):
+    feat, tok = lax.axis_size("feat"), lax.axis_size("tok")
+    tokens, width = activations.shape
+    tiles, quarter, _ = hessian.shape
+    any_space = pl.BlockSpec(memory_space=pl.ANY)
+    dma = pltpu.SemaphoreType.DMA
+    cols, rows = pl.pallas_call(
+        lambda *refs: share_kernel(feat, tok, *refs),
+        out_shape=(
+            jax.ShapeDtypeStruct((feat, quarter, tok * tokens), activations.dtype),
+            jax.ShapeDtypeStruct((tok * tokens, width), activations.dtype),
+        ),
+        in_specs=[any_space] * 2,
+        out_specs=(any_space, any_space),
+        scratch_shapes=[dma((feat, tok)), dma((feat, tok)), dma((tok,)), dma((feat, tok)),
+                        dma((3,)), dma((tok,)), dma((2,))],
+        compiler_params=pltpu.CompilerParams(collective_id=0, has_side_effects=True),
+        name="share",
+    )(activations, activations.T)
+    seen_share, weight_new = shares(activations)
+    pos = jnp.stack([lax.axis_index("feat"), lax.axis_index("tok")]).astype(jnp.int32)
+    tile = pl.BlockSpec((1, quarter, width), lambda j, pos: (j, 0, 0))
+    return pl.pallas_call(
+        lambda *refs: blend_kernel(seen_share, weight_new, *refs),
+        out_shape=jax.ShapeDtypeStruct(hessian.shape, hessian.dtype),
+        grid_spec=pltpu.PrefetchScalarGridSpec(
+            num_scalar_prefetch=1,
+            grid=(tiles,),
+            in_specs=[
+                pl.BlockSpec((1, quarter, tok * tokens),
+                             lambda j, pos: (jnp.minimum(j, pos[0]), 0, 0)),
+                pl.BlockSpec((tok * tokens, width), lambda j, pos: (0, 0),
+                             pipeline_mode=pl.Buffered(1)),
+                tile,
+            ],
+            out_specs=tile,
+        ),
+        compiler_params=pltpu.CompilerParams(vmem_limit_bytes=48 * 1024 * 1024),
+        name="blend",
+    )(pos, cols, rows, hessian)
+
+
+def on_device(activations, hessian):
+    tokens, width = activations.shape
+    whole_panels = (
+        lax.axis_size("feat") == TILES
+        and lax.axis_size("tok") == 4
+        and hessian.shape[0] == TILES
+        and hessian.shape[2] == width
+        and width % 128 == 0
+        and hessian.shape[1] % 16 == 0
+        and tokens % 128 == 0
+    )
+    return (on_device_panels if whole_panels else on_device_general)(activations, hessian)
+
+
 def solution(mesh):
     in_specs = (P("tok", "feat"), P("feat", "tok", None))
     out_specs = P("feat", "tok", None)

time: 1060 us -> 297 us (0.28)
  waiting for transfers between devices: 601 us -> 0 us
  Pallas kernels: 0 us -> 293 us
  blocking collectives: 243 us -> 0 us
  matrix products: 86.6 us -> 0 us
  local copies, waits for them, and re-layouts: 73.1 us -> 4.06 us
  other arithmetic: 21.8 us -> 0.07 us
  between operations: 14.1 us -> 0.01 us
  starting transfers between devices: 12.9 us -> 0 us
    all_gather x9 -> x0, waiting for transfers between devices: 505 us -> none  [the longest x1 328 us: on_device(): gathered = lax.all_gather(activations, 'feat', axis=1, tiled=True)]
    pallas_call x0 -> x2, Pallas kernels: none -> 293 us  [the longest x1 245 us: on_device_panels(): pl.pallas_call(lambda *refs: share_kernel(feat, tok, *refs), out_shape=(j...]
    all_to_all x5 -> x0, blocking collectives: 243 us -> none  [tile_sums(): lax.all_to_all(col_block, 'tok', split_axis=1, concat_axis=0, tiled=True)]
    all_to_all x3 -> x0, waiting for transfers between devices: 91.5 us -> none  [tile_sums(): lax.all_to_all(col_block, 'tok', split_axis=1, concat_axis=0, tiled=True)]
    dot_general x8 -> x0, matrix products: 86.6 us -> none  [contract_tokens(): lax.dot_general(left, right, (((0,), (0,)), ((), ())), preferred_element_...]
    another operation x8 -> x0, local copies, waits for them, and re-layouts: 34.4 us -> none
    dynamic_slice x1 -> x0, local copies, waits for them, and re-layouts: 25.9 us -> none  [on_device(): row_block = lax.dynamic_slice_in_dim(gathered, row_tile * width, width, 1)]
    unnamed x7 -> x0, other arithmetic: 17.9 us -> none
  transfers between devices with their start and end apart: 12 -> 0, of which waited for: 7 -> 0; matrix products, arithmetic and copies ran while one was open for 10% -> 0% of each run, Pallas kernels for 0% -> 0%
where the time goes in v1:
time: 297 us
  Pallas kernels  293 us (99%)
  local copies, waits for them, and re-layouts  4.06 us (1%)
    pallas_call x1, Pallas kernels, on_device_panels(): pl.pallas_call(lambda *refs: share_kernel(feat, tok, *refs), out_shape=(j...  245 us
    pallas_call x1, Pallas kernels, on_device_panels(): pl.pallas_call(lambda *refs: blend_kernel(seen_share, weight_new, *refs),...  47.9 us

profile of v1, /device:TPU:28, one launch (start us, length us, event | category | flops | bytes accessed | tf_op | source)
XLA Modules:
  0.0 296.9 jit_solution(2938080634884995950)
XLA Ops:
  0.0 0.1 pad_add_fusion.refs_0_
  0.1 4.1 %copy.3 = bf16[640,1664]{0,1:T(8,128)(2,1)} copy(bf16[640,1664]{1,0:T(8,128)(2,1)} %refs_0_.1) | data formatting | bytes 4259840 | tf_op args[0]
  4.1 244.8 %share.1 = (bf16[8,416,2560]{2,1,0:T(8,128)(2,1)}, bf16[2560,1664]{1,0:T(8,128)(2,1)}) custom-call(bf16[640,1664]{1,0:T(8,128)(2,1)} %refs_0_.1, bf16[1664,640]{1,0:T(8,128)(2,1)} %bitcast.3), custom_call_target="tpu_custom_call" | custom-call | tf_op jit(solution)/shard_map/share/pallas_call | solution.py:237
  249.0 47.9 %blend.1 = f32[8,416,1664]{2,1,0:T(8,128)} custom-call(s32[2]{0:T(128)S(1)} %pad_add_fusion.refs_0_, bf16[8,416,2560]{2,1,0:T(8,128)(2,1)} %get-tuple-element.7.refs_1_, bf16[2560,1664]{1,0:T(8,128)(2,1)} %get-tuple-element.8.refs_2_, f32[8,416,1664]{2,1,0:T(8,128)} %refs_3_.1), custom_call_target="tpu_custom_call" | custom-call | tf_op jit(solution)/shard_map/blend/pallas_call | solution.py:253

commit v2 on v1

--- a/solution.py
+++ b/solution.py
@@ -120,10 +120,9 @@
             copy.start()
         ended.append((cond, copy))
 
-    def lane(even, r, j):
-        if even:
-            return r % 2 + 0 * j
-        return jnp.where((r == 3) | ((r == 2) & (j == feat - 3)), 0, 1)
+    def lane(r, j):
+        odd_lane = jnp.where((r == 3) | ((r == 2) & (j > 1)), 0, 1)
+        return jnp.where(j % 2 == 0, r % 2, odd_lane)
 
     def forward_up(j, r, lane_of, src=None):
         src = block(j, near[r]) if src is None else src
@@ -134,30 +133,52 @@
         copy.start()
     own_cols = pltpu.make_async_copy(mine(t), block(p, t), local_sem.at[0])
     own_rows = pltpu.make_async_copy(a_ref, row_block(t), local_sem.at[1])
-    own_lane = [jnp.where(y == 0, r % 2, lane(False, r, p)) for r in range(4)]
-    side_lane = [jnp.where(y == 1, r % 2, lane(False, r, side)) for r in range(4)]
     row_sends = [send_row(a_ref, t, 0, (p, near[2])), send_row(a_ref, t, 1, (p, near[1]))]
 
-    for r in range(4):
+    def own_block(r):
         if r:
             arrive(p, r)
-        src = mine(t) if r == 0 else None
-        forward_up(p, r, own_lane[r], src)
-        start_if((y == 0) | (has_up & (own_lane[r] == 0)),
-                 move(block(p, near[r]) if src is None else src, p, near[r],
-                      side_sem.at[p, r], (side, t)))
-        if r == 0:
-            own_cols.start()
-            own_rows.start()
-        if r == 1:
-            for copy in row_sends:
-                copy.start()
-
-    for r in range(4):
-        @pl.when((y == 1) | (has_up & (side_lane[r] == 0)))
+        src = mine(t) if r == 0 else block(p, near[r])
+        forward_up(p, r, lane(r, p), src)
+        start_if((y == 0) | (has_up & (lane(r, p) == 0)),
+                 move(src, p, near[r], side_sem.at[p, r], (side, t)))
+
+    def side_block(r):
+        @pl.when(has_up & ((y == 1) | (lane(r, side) == 0)))
         def _():
             arrive(side, r)
-        forward_up(side, r, side_lane[r])
+        forward_up(side, r, lane(r, side))
+
+    def pass_block(dz, first, r):
+        j = jnp.maximum(2 * (z - dz) + (y if first else 1 - y), 0)
+        cond = (z >= dz) & (lane(r, j) == y)
+
+        @pl.when(cond)
+        def _():
+            arrive(j, r)
+        start_if(cond & has_up, move(block(j, near[r]), j, near[r], up_sem.at[j, r], (up, t)))
+        start_if(cond, move(block(j, near[r]), j, near[r], side_sem.at[j, r], (side, t)))
+
+    own_block(0)
+    own_cols.start()
+    own_rows.start()
+    first_cond, first_copy = ended.pop(0)
+
+    @pl.when(first_cond)
+    def _():
+        first_copy.wait_send()
+
+    own_block(1)
+    side_block(0)
+    side_block(1)
+    pass_block(1, True, 0)
+    pass_block(1, True, 1)
+    own_block(2)
+    own_block(3)
+    for copy in row_sends:
+        copy.start()
+    side_block(2)
+    side_block(3)
 
     pass_row = send_row(row_block(near[2]), near[2], 2, (p, near[1]))
 
@@ -167,28 +188,26 @@
 
     own_rows.wait()
     for dz in range(1, last_z + 1):
-        for even in (True, False):
+        for first in (True, False):
             for r in range(4):
-                j = jnp.maximum(2 * (z - dz) + (0 if even else 1), 0)
-                here = lane(even, r, j) == y
-                cond = (z >= dz) & here
-
-                @pl.when(cond)
+                if (dz, first, r) not in ((1, True, 0), (1, True, 1)):
+                    pass_block(dz, first, r)
+        if dz == max(last_z - 1, 1):
+            pass_rows()
+
+    for dz in range(1, last_z + 1):
+        for k in (0, 1):
+            for r in range(4):
+                j = jnp.maximum(2 * (z - dz) + k, 0)
+
+                @pl.when((z >= dz) & (lane(r, j) != y))
                 def _():
                     arrive(j, r)
-                start_if(cond & has_up, move(block(j, near[r]), j, near[r], up_sem.at[j, r], (up, t)))
-                start_if(cond, move(block(j, near[r]), j, near[r], side_sem.at[j, r], (side, t)))
-        if dz == 1:
-            pass_rows()
-
-    for dz in range(1, last_z + 1):
-        for even in (True, False):
-            for r in range(4):
-                j = jnp.maximum(2 * (z - dz) + (0 if even else 1), 0)
-
-                @pl.when((z >= dz) & (lane(even, r, j) != y))
-                def _():
-                    arrive(j, r)
+
+    for r in range(4):
+        @pl.when((z == last_z) & (y == 1))
+        def _():
+            arrive(side, r)
 
     for r in (1, 3):
         send_row(row_block(near[r]), near[r], 2, (p, near[1])).wait_recv()
@@ -217,11 +236,8 @@
     @pl.when(j <= pos[0])
     def _():
         step = 256
-        @pl.loop(0, width // step)
-        def _(i):
-            part(pl.multiple_of(i * step, step), step)
-        if width % step:
-            part(width // step * step, width % step)
+        for start in range(0, width, step):
+            part(start, min(step, width - start))
 
     @pl.when(j > pos[0])
     def _():

time: 297 us -> 256 us (0.86)
  Pallas kernels: 293 us -> 251 us
    pallas_call x1, Pallas kernels: 245 us -> 211 us  [on_device_panels(): pl.pallas_call(lambda *refs: share_kernel(feat, tok, *refs), out_shape=(j...]
    pallas_call x1, Pallas kernels: 47.9 us -> 40.7 us  [on_device_panels(): pl.pallas_call(lambda *refs: blend_kernel(seen_share, weight_new, *refs),...]
where the time goes in v2:
time: 256 us; the launch traced here: 255 us
  Pallas kernels  251 us (98%)
  local copies, waits for them, and re-layouts  4.06 us (2%)
    pallas_call x1, Pallas kernels, on_device_panels(): pl.pallas_call(lambda *refs: share_kernel(feat, tok, *refs), out_shape=(j...  211 us
    pallas_call x1, Pallas kernels, on_device_panels(): pl.pallas_call(lambda *refs: blend_kernel(seen_share, weight_new, *refs),...  40.7 us

profile of v2, /device:TPU:28, one launch (start us, length us, event | category | flops | bytes accessed | tf_op | source)
XLA Modules:
  0.0 255.4 jit_solution(148946315132430432)
XLA Ops:
  0.0 0.1 pad_add_fusion.refs_0_
  0.1 4.1 %copy.3 = bf16[640,1664]{0,1:T(8,128)(2,1)} copy(bf16[640,1664]{1,0:T(8,128)(2,1)} %refs_0_.1) | data formatting | bytes 4259840 | tf_op args[0]
  4.1 210.6 %share.1 = (bf16[8,416,2560]{2,1,0:T(8,128)(2,1)}, bf16[2560,1664]{1,0:T(8,128)(2,1)}) custom-call(bf16[640,1664]{1,0:T(8,128)(2,1)} %refs_0_.1, bf16[1664,640]{1,0:T(8,128)(2,1)} %bitcast.3), custom_call_target="tpu_custom_call" | custom-call | tf_op jit(solution)/shard_map/share/pallas_call | solution.py:253
  214.7 40.7 %blend.1 = f32[8,416,1664]{2,1,0:T(8,128)} custom-call(s32[2]{0:T(128)S(1)} %pad_add_fusion.refs_0_, bf16[8,416,2560]{2,1,0:T(8,128)(2,1)} %get-tuple-element.7.refs_1_, bf16[2560,1664]{1,0:T(8,128)(2,1)} %get-tuple-element.8.refs_2_, f32[8,416,1664]{2,1,0:T(8,128)} %refs_3_.1), custom_call_target="tpu_custom_call" | custom-call | tf_op jit(solution)/shard_map/blend/pallas_call | solution.py:269
